TPU v7x, 128 devices: a whole 4x4x4 slice. The times are simulated.
128 devices in a mesh: blk: 16 (over x, z), grp: 8 (over y, core).
Axes of the slice: x: 4, y: 4, z: 4, core: 2. Of those that a mesh axis runs over, the one named last changes fastest.
Arguments:
- snapshots: bfloat16 [262144, 1024], P(('grp', 'blk')), may hold values from -1200 to 1200
- start: float32 [1024, 256], replicated, may hold values from -6 to 6
- pivot_dev: int32 [32], replicated, may hold values from 0 to 127, as said below
- pivot_row: int32 [32], replicated, may hold values from 0 to 2047, as said below
Outputs:
- modes: bfloat16 [262144, 256], P(('grp', 'blk'))
- scores: float32 [262144], P(('grp', 'blk'))
- panel_basis: float32 [256, 32], replicated
Inputs may be any that keep to these rules, and one draw needn't show every extreme that they name: Together with pivot_row, names 32 distinct global rows pivot_dev * 2048 + pivot_row; the first and the last global row are always among them. `pivot_row`: see pivot_dev.
All inputs are finite; a program needn't handle non-finite values.
Results may differ from a plain program's by a relative error of at most 0.0051.
Values sent between devices are 32-bit elements; how exact they have to be, the bound alone decides.
A program may use at most 64 MiB of HBM per device.

v0:
```python
import jax
import jax.numpy as jnp
from jax import lax
from jax.sharding import Mesh
from jax.sharding import PartitionSpec as P

ITERS = 4
GRP_BLK = ("grp_0", "grp_1", "blk_0", "blk_1")


def over_axes(array, axes):
    for axis in axes:
        array = lax.psum(array, axis)
    return array


def right_solve(factor, matrix):
    return lax.linalg.triangular_solve(
        factor, matrix, left_side=False, lower=True, transpose_a=True
    )


def local(snapshots, start, pivot_dev, pivot_row):
    local_gram = lax.dot_general(
        snapshots, snapshots, (((0,), (0,)), ((), ())), preferred_element_type=jnp.float32
    )
    rows_total = snapshots.shape[0] * lax.axis_size(GRP_BLK)
    gram_full = lax.psum(local_gram, GRP_BLK)

    def apply_gram(iterate):
        return jnp.dot(gram_full, iterate, precision=lax.Precision.HIGHEST)

    iterate = start
    for repeat in range(ITERS):
        image = apply_gram(iterate)
        square = jnp.dot(image.T, image, precision=lax.Precision.HIGHEST)
        iterate = right_solve(jnp.linalg.cholesky(square), image)
    image = apply_gram(iterate)
    small_gram = jnp.dot(iterate.T, image, precision=lax.Precision.HIGHEST) / rows_total
    coef = right_solve(jnp.linalg.cholesky(small_gram), iterate).astype(jnp.bfloat16)
    basis = jnp.dot(snapshots, coef, preferred_element_type=jnp.float32)
    myself = lax.axis_index(GRP_BLK)
    picked = basis[pivot_row]
    owned = (pivot_dev == myself)[:, None]
    panel = over_axes(jnp.where(owned, picked, 0.0), GRP_BLK)
    panel_gram = jnp.dot(panel, panel.T, precision=lax.Precision.HIGHEST)
    panel_basis = right_solve(jnp.linalg.cholesky(panel_gram), panel.T)
    coeffs = jnp.dot(basis, panel_basis, precision=lax.Precision.HIGHEST)
    remaining = basis - jnp.dot(coeffs, panel_basis.T, precision=lax.Precision.HIGHEST)
    scores = jnp.sum(remaining * remaining, axis=1) / basis.shape[1]
    return (basis.astype(jnp.bfloat16), scores, panel_basis)


def solution(mesh):
    torus = Mesh(mesh.devices.reshape(4, 4, 4, 2), ("blk_0", "blk_1", "grp_0", "grp_1"))
    placed = (P(GRP_BLK, None), P(), P(), P())
    return jax.shard_map(
        local,
        mesh=torus,
        in_specs=placed,
        out_specs=(P(GRP_BLK, None), P(GRP_BLK), P()),
        check_vma=False,
    )
```

profile of v0, /device:TPU:1, one launch (start us, length us, event | category | flops | bytes accessed | tf_op | source)
XLA Modules:
  0.0 613.6 jit_solution(9730837904440173774)
XLA Ops:
  7.2 10.1 %fusion.87 = f32[1024,1024]{1,0:T(8,128)} fusion(bf16[2048,1024]{1,0:T(8,128)(2,1)} %param.7), kind=kOutput, calls=%fused_computation.175 | convolution fusion | flops 4294967296 | bytes 8388608 | tf_op jit(solution)/shard_map/dot_general | solution.py:24
  18.0 156.8 %all-reduce.3.cloned.1.call-done = f32[1024,1024]{1,0:T(8,128)} async-done(((f32[1024,1024]{1,0:T(8,128)}), f32[1024,1024]{1,0:T(8,128)}) %all-reduce.3.cloned.1.call-update) | async-done | bytes 4194320 | tf_op jit(solution)/shard_map/psum | solution.py:28
  182.3 11.7 %cholesky.291 = f32[128,128]{1,0:T(8,128)S(1)} custom-call(f32[128,128]{1,0:T(8,128)S(1)} %cholesky.457), custom_call_target="Cholesky" | custom-call | tf_op jit(solution)/shard_map/jit(cholesky)/cholesky | solution.py:37
  194.0 9.8 %custom-call.26 = f32[1,128,128]{1,2,0:T(8,128)S(1)} custom-call(f32[1,128,128]{2,1,0:T(8,128)S(1)} %get-tuple-element.114), custom_call_target="InvertDiagBlocksLowerTriangular" | custom-call | tf_op jit(solution)/shard_map/jit(cholesky)/cholesky | solution.py:37
  204.4 11.7 %cholesky.308 = f32[128,128]{1,0:T(8,128)S(1)} custom-call(f32[128,128]{1,0:T(8,128)S(1)} %convolution_subtract_fusion.10), custom_call_target="Cholesky" | custom-call | tf_op jit(solution)/shard_map/jit(cholesky)/cholesky | solution.py:37
  234.9 19.7 %custom-call.27 = f32[2,128,128]{1,2,0:T(8,128)S(1)} custom-call(f32[2,128,128]{2,1,0:T(8,128)S(1)} %get-tuple-element.37), custom_call_target="InvertDiagBlocksLowerTriangular" | custom-call | tf_op jit(solution)/shard_map/triangular_solve/custom-call.4 | solution.py:18
  264.3 11.7 %cholesky.325 = f32[128,128]{1,0:T(8,128)S(1)} custom-call(f32[128,128]{1,0:T(8,128)S(1)} %cholesky.460), custom_call_target="Cholesky" | custom-call | tf_op jit(solution)/shard_map/jit(cholesky)/cholesky | solution.py:37
  276.1 9.8 %custom-call.28 = f32[1,128,128]{1,2,0:T(8,128)S(1)} custom-call(f32[1,128,128]{2,1,0:T(8,128)S(1)} %get-tuple-element.110), custom_call_target="InvertDiagBlocksLowerTriangular" | custom-call | tf_op jit(solution)/shard_map/jit(cholesky)/cholesky | solution.py:37
  286.4 11.7 %cholesky.342 = f32[128,128]{1,0:T(8,128)S(1)} custom-call(f32[128,128]{1,0:T(8,128)S(1)} %convolution_subtract_fusion.9), custom_call_target="Cholesky" | custom-call | tf_op jit(solution)/shard_map/jit(cholesky)/cholesky | solution.py:37
  305.1 19.7 %custom-call.29 = f32[2,128,128]{1,2,0:T(8,128)S(1)} custom-call(f32[2,128,128]{2,1,0:T(8,128)S(1)} %get-tuple-element.38), custom_call_target="InvertDiagBlocksLowerTriangular" | custom-call | tf_op jit(solution)/shard_map/triangular_solve/custom-call.4 | solution.py:18
  334.7 11.7 %cholesky.359 = f32[128,128]{1,0:T(8,128)S(1)} custom-call(f32[128,128]{1,0:T(8,128)S(1)} %cholesky.463), custom_call_target="Cholesky" | custom-call | tf_op jit(solution)/shard_map/jit(cholesky)/cholesky | solution.py:37
  346.4 9.8 %custom-call.30 = f32[1,128,128]{1,2,0:T(8,128)S(1)} custom-call(f32[1,128,128]{2,1,0:T(8,128)S(1)} %get-tuple-element.106), custom_call_target="InvertDiagBlocksLowerTriangular" | custom-call | tf_op jit(solution)/shard_map/jit(cholesky)/cholesky | solution.py:37
  356.7 11.7 %cholesky.376 = f32[128,128]{1,0:T(8,128)S(1)} custom-call(f32[128,128]{1,0:T(8,128)S(1)} %convolution_subtract_fusion.8), custom_call_target="Cholesky" | custom-call | tf_op jit(solution)/shard_map/jit(cholesky)/cholesky | solution.py:37
  375.3 19.7 %custom-call.31 = f32[2,128,128]{1,2,0:T(8,128)S(1)} custom-call(f32[2,128,128]{2,1,0:T(8,128)S(1)} %get-tuple-element.39), custom_call_target="InvertDiagBlocksLowerTriangular" | custom-call | tf_op jit(solution)/shard_map/triangular_solve/custom-call.4 | solution.py:18
  405.1 11.7 %cholesky.393 = f32[128,128]{1,0:T(8,128)S(1)} custom-call(f32[128,128]{1,0:T(8,128)S(1)} %cholesky.466), custom_call_target="Cholesky" | custom-call | tf_op jit(solution)/shard_map/jit(cholesky)/cholesky | solution.py:37
  427.2 11.7 %cholesky.410 = f32[128,128]{1,0:T(8,128)S(1)} custom-call(f32[128,128]{1,0:T(8,128)S(1)} %convolution_subtract_fusion.7), custom_call_target="Cholesky" | custom-call | tf_op jit(solution)/shard_map/jit(cholesky)/cholesky | solution.py:37
  445.8 19.7 %custom-call.33 = f32[2,128,128]{1,2,0:T(8,128)S(1)} custom-call(f32[2,128,128]{2,1,0:T(8,128)S(1)} %get-tuple-element.40), custom_call_target="InvertDiagBlocksLowerTriangular" | custom-call | tf_op jit(solution)/shard_map/triangular_solve/custom-call.4 | solution.py:18
  475.1 11.7 %cholesky.427 = f32[128,128]{1,0:T(8,128)S(1)} custom-call(f32[128,128]{1,0:T(8,128)S(1)} %cholesky.469), custom_call_target="Cholesky" | custom-call | tf_op jit(solution)/shard_map/jit(cholesky)/cholesky | solution.py:40
  486.9 9.8 %custom-call.34 = f32[1,128,128]{1,2,0:T(8,128)S(1)} custom-call(f32[1,128,128]{2,1,0:T(8,128)S(1)} %get-tuple-element.98), custom_call_target="InvertDiagBlocksLowerTriangular" | custom-call | tf_op jit(solution)/shard_map/jit(cholesky)/cholesky | solution.py:40
  497.2 11.7 %cholesky.444 = f32[128,128]{1,0:T(8,128)S(1)} custom-call(f32[128,128]{1,0:T(8,128)S(1)} %convolution_subtract_fusion.6), custom_call_target="Cholesky" | custom-call | tf_op jit(solution)/shard_map/jit(cholesky)/cholesky | solution.py:40
  515.8 19.7 %custom-call.35 = f32[2,128,128]{1,2,0:T(8,128)S(1)} custom-call(f32[2,128,128]{2,1,0:T(8,128)S(1)} %get-tuple-element.41), custom_call_target="InvertDiagBlocksLowerTriangular" | custom-call | tf_op jit(solution)/shard_map/triangular_solve/custom-call.4 | solution.py:18
  545.9 12.8 %psum.36 = f32[32,256]{1,0:T(8,128)S(1)} all-reduce(f32[32,256]{1,0:T(8,128)S(1)} %broadcast_select_fusion), channel_id=1, replica_groups=mesh['blk_0'=4,'blk_1'=4,'grp_0'=4,'grp_1'=2] {'grp_0'}, use_global_device_ids=true, to_apply=%region_5.8 | all-reduce | flops 8192 | bytes 65536 | tf_op jit(solution)/shard_map/psum | solution.py:13
  566.0 13.3 %psum.38 = f32[32,256]{1,0:T(8,128)S(1)} all-reduce(f32[32,256]{1,0:T(8,128)S(1)} %psum.37), channel_id=1, replica_groups=mesh['blk_0'=4,'blk_1'=4,'grp_0'=4,'grp_1'=2] {'blk_0'}, use_global_device_ids=true, to_apply=%region_7.10 | all-reduce | flops 8192 | bytes 65536 | tf_op jit(solution)/shard_map/psum | solution.py:13
  579.3 11.5 %psum.39 = f32[32,256]{1,0:T(8,128)S(1)} all-reduce(f32[32,256]{1,0:T(8,128)S(1)} %psum.38), channel_id=1, replica_groups=mesh['blk_0'=4,'blk_1'=4,'grp_0'=4,'grp_1'=2] {'blk_1'}, use_global_device_ids=true, to_apply=%region_8.11 | all-reduce | flops 8192 | bytes 65536 | tf_op jit(solution)/shard_map/psum | solution.py:13
  (153 shorter events, 139.6 us)
Async XLA Ops:
  7.2 167.6 %copy-start = (f32[1024,256]{1,0:T(8,128)S(1)}, f32[1024,256]{1,0:T(8,128)}, u32[]{:S(2)}) copy-start(f32[1024,256]{1,0:T(8,128)} %param.8) | copy-start | bytes 3145732
  7.2 167.6 %all-reduce.3.cloned.1.call-start = ((), (), s32[]{:S(2)}) async-start(), calls=%async_computation | async-start | bytes 8388608 | tf_op jit(solution)/shard_map/psum | solution.py:28
  17.3 0.7 copy-start.2
  17.3 0.7 copy-start.3
  598.0 8.3 %copy-start.1 = (f32[256,32]{0,1:T(8,128)}, f32[256,32]{0,1:T(8,128)S(1)}, u32[]{:S(2)}) copy-start(f32[256,32]{0,1:T(8,128)S(1)} %fusion.72) | copy-start | bytes 98308
Sparse Core Ops, SparseCore 0:
  17.4 157.2 all-reduce.2
where the time goes:
time: 625 us; the launch traced here: 614 us
  other arithmetic  279 us (45%)
  waiting for transfers between devices  157 us (25%)
  matrix products  70.2 us (11%)
  blocking collectives  44.8 us (7%)
  between operations  34.5 us (6%)
  local copies, waits for them, and re-layouts  27.6 us (4%)
    psum x1, waiting for transfers between devices, local(): gram_full = lax.psum(local_gram, GRP_BLK)  157 us
    another operation x27, other arithmetic, local(): iterate = right_solve(jnp.linalg.cholesky(square), image)  138 us
    another operation x13, other arithmetic, right_solve(): lax.linalg.triangular_solve(factor, matrix, left_side=False, lower=True,...  103 us
    psum x4, blocking collectives, over_axes(): array = lax.psum(array, axis)  44.8 us
    another operation x7, other arithmetic, local(): jnp.linalg.cholesky(small_gram)  34.6 us
    dot_general x5, matrix products, apply_gram(): return jnp.dot(gram_full, iterate, precision=lax.Precision.HIGHEST)  27.4 us
    another operation x36, local copies, waits for them, and re-layouts, right_solve(): lax.linalg.triangular_solve(factor, matrix, left_side=False, lower=True,...  19.8 us
  transfers between devices with their start and end apart: 1, of which 1 were waited for; matrix products, arithmetic and copies ran while one was open for 0% of the time, Pallas kernels for 0%

commit v1 on v0

v1 whole, which is shorter than its diff:
```python
import functools
import jax, jax.numpy as jnp
from jax import lax
from jax.experimental import pallas as pl
from jax.experimental.pallas import tpu as pltpu
from jax.sharding import Mesh
from jax.sharding import PartitionSpec as P

MESH = pl.DeviceIdType.MESH
F32, BF16 = jnp.float32, jnp.bfloat16
NB = 64
NJ = 4
PAIRS = [(0, 0), (0, 1), (0, 2), (0, 3), (1, 1), (1, 2), (1, 3), (2, 2), (2, 3), (3, 3)]

NN = (((1,), (0,)), ((), ()))
NT = (((1,), (1,)), ((), ()))


def split(x):
    hi = x.astype(BF16)
    return hi, (x - hi.astype(F32)).astype(BF16)


def dot(a, b, dims):
    return lax.dot_general(a, b, dims, preferred_element_type=F32)


def dot3(a, b, dims):
    return dot(a[0], b[0], dims) + (dot(a[0], b[1], dims) + dot(a[1], b[0], dims))


AXES = ("x", "z", "y", "core")
TURNS = (("x", "y", "z"), ("y", "z", "x"), ("z", "x", "y"))


def reduce_kernel(x_ref, pdev_ref, prow_ref, out_ref, loc, r0, acc, r1, a1, r2, a2, r3,
                  send0, recv0, send_down, recv_down, send_up, recv_up, send4, recv4):
    at = {name: lax.axis_index(name) for name in AXES}
    core = at["core"]
    other = 1 - core

    barrier = pltpu.get_barrier_semaphore()
    pl.semaphore_signal(barrier, inc=1, device_id={"core": other}, device_id_type=MESH)
    for axis in ("x", "y", "z"):
        for d in (1, 2, 3):
            pl.semaphore_signal(barrier, inc=1, device_id={axis: lax.rem(at[axis] + d, 4)}, device_id_type=MESH)
    pl.semaphore_wait(barrier, 10)

    def remote(src, dst, send, recv, axis, position):
        return pltpu.make_async_remote_copy(src_ref=src, dst_ref=dst, send_sem=send, recv_sem=recv,
                                            device_id={axis: position}, device_id_type=MESH)

    sent = []

    def go(copy):
        copy.start()
        sent.append(copy)
        return copy

    swaps = {}

    def pair(m):
        for half in (0, 1):
            n = 2 * m + half
            if n < 10:
                i, j = PAIRS[n]
                loc[m, half] = lax.dot_general(x_ref[:, 256 * i:256 * i + 256], x_ref[:, 256 * j:256 * j + 256],
                                               (((0,), (0,)), ((), ())), preferred_element_type=F32)
            elif n == 10:
                me = ((at["y"] * 2 + core) * 4 + at["x"]) * 4 + at["z"]
                where = lax.broadcasted_iota(jnp.int32, (32, 2048), 1)
                hit = (where == prow_ref[...]) & (pdev_ref[...] == me)
                picked = dot(hit.astype(F32).astype(BF16), x_ref[...], NN)
                for part in range(4):
                    loc[m, half, 32 * part:32 * part + 32, :] = picked[:, 256 * part:256 * part + 256]
                loc[m, half, 128:256, :] = jnp.zeros((128, 256), F32)
            else:
                loc[m, half] = jnp.zeros((256, 256), F32)
        swaps[m] = go(remote(loc.at[m, other], r0.at[m], send0.at[m], recv0.at[m], "core", other))

    def offsets(axis):
        return [(d, lax.rem(at[axis] + d, 4)) for d in (1, 2, 3)]

    down, up = {}, {}

    def down1(c):
        for m in (2 * c, 2 * c + 1):
            swaps[m].wait_recv()
            total = loc[m, core] + r0[m]
            acc[c, 2 * (m % 2)] = total[:128]
            acc[c, 2 * (m % 2) + 1] = total[128:]
        axis = TURNS[c][0]
        down[0, c] = [go(remote(acc.at[c, p], r1.at[c, d - 1], send_down.at[0, c, d - 1], recv_down.at[0, c, d - 1], axis, p))
                      for d, p in offsets(axis)]

    def down2(c):
        for copy in down[0, c]:
            copy.wait_recv()
        total = (acc[c, at[TURNS[c][0]]] + r1[c, 0]) + (r1[c, 1] + r1[c, 2])
        for i in range(4):
            a1[c, i] = total[32 * i:32 * i + 32]
        axis = TURNS[c][1]
        down[1, c] = [go(remote(a1.at[c, p], r2.at[c, d - 1], send_down.at[1, c, d - 1], recv_down.at[1, c, d - 1], axis, p))
                      for d, p in offsets(axis)]

    def down3(c):
        for copy in down[1, c]:
            copy.wait_recv()
        total = (a1[c, at[TURNS[c][1]]] + r2[c, 0]) + (r2[c, 1] + r2[c, 2])
        for i in range(4):
            a2[c, i] = total[8 * i:8 * i + 8]
        axis = TURNS[c][2]
        down[2, c] = [go(remote(a2.at[c, p], r3.at[c, d - 1], send_down.at[2, c, d - 1], recv_down.at[2, c, d - 1], axis, p))
                      for d, p in offsets(axis)]

    def up3(c):
        for copy in down[2, c]:
            copy.wait_recv()
        one, two, three = (at[name] for name in TURNS[c])
        out_ref[core, c, one, two, three] = (a2[c, three] + r3[c, 0]) + (r3[c, 1] + r3[c, 2])
        mine = out_ref.at[core, c, one, two, three]
        axis = TURNS[c][2]
        up[2, c] = [go(remote(mine, mine, send_up.at[2, c, d - 1], recv_up.at[2, c, d - 1], axis, p)) for d, p in offsets(axis)]

    def up2(c):
        for copy in up[2, c]:
            copy.wait_recv()
        one, two, three = (at[name] for name in TURNS[c])
        mine = out_ref.at[core, c, one, two]
        axis = TURNS[c][1]
        up[1, c] = [go(remote(mine, mine, send_up.at[1, c, d - 1], recv_up.at[1, c, d - 1], axis, p)) for d, p in offsets(axis)]

    def up1(c):
        for copy in up[1, c]:
            copy.wait_recv()
        one, two, three = (at[name] for name in TURNS[c])
        mine = out_ref.at[core, c, one]
        axis = TURNS[c][0]
        up[0, c] = [go(remote(mine, mine, send_up.at[0, c, d - 1], recv_up.at[0, c, d - 1], axis, p)) for d, p in offsets(axis)]

    def last(c):
        for copy in up[0, c]:
            copy.wait_recv()
        mine = out_ref.at[core, c]
        up[3, c] = go(remote(mine, mine, send4.at[c], recv4.at[c], "core", other))

    pair(0)
    pair(1)
    pair(2)
    pair(3)
    down1(0)
    pair(4)
    pair(5)
    down1(1)
    down1(2)
    for stage in (down2, down3, up3, up2, up1, last):
        for c in range(3):
            stage(c)
    for c in range(3):
        up[3, c].wait_recv()
    for copy in sent:
        copy.wait_send()


def reduce_call(x, pdev, prow):
    return pl.pallas_call(
        reduce_kernel,
        out_shape=jax.ShapeDtypeStruct((2, 3, 4, 4, 4, 8, 256), F32),
        in_specs=[pl.BlockSpec(memory_space=pltpu.VMEM)] * 3,
        out_specs=pl.BlockSpec(memory_space=pltpu.VMEM),
        scratch_shapes=[
            pltpu.VMEM((6, 2, 256, 256), F32), pltpu.VMEM((6, 256, 256), F32), pltpu.VMEM((3, 4, 128, 256), F32),
            pltpu.VMEM((3, 3, 128, 256), F32), pltpu.VMEM((3, 4, 32, 256), F32),
            pltpu.VMEM((3, 3, 32, 256), F32), pltpu.VMEM((3, 4, 8, 256), F32), pltpu.VMEM((3, 3, 8, 256), F32),
            pltpu.SemaphoreType.DMA((6,)), pltpu.SemaphoreType.DMA((6,)),
            pltpu.SemaphoreType.DMA((3, 3, 3)), pltpu.SemaphoreType.DMA((3, 3, 3)),
            pltpu.SemaphoreType.DMA((3, 3, 3)), pltpu.SemaphoreType.DMA((3, 3, 3)),
            pltpu.SemaphoreType.DMA((3,)), pltpu.SemaphoreType.DMA((3,)),
        ],
        compiler_params=pltpu.CompilerParams(vmem_limit_bytes=48 * 1024 * 1024, collective_id=0, has_side_effects=True),
        name="gram_sum",
    )(x, pdev, prow)


def inverse_factors(s_ref, o_ref, panels, first):
    rows_of = lambda i: pl.ds(8 * i, 8)
    spread = lambda row, c: jnp.broadcast_to(row[:, c:c + 1], (8, 128))
    for p in range(panels):
        rows = [s_ref[rows_of(8 * p + r), :] for r in range(8)]
        e = [[spread(rows[r], first + 8 * p + c) if c >= r else None for c in range(8)] for r in range(8)]
        for r in range(8):
            g = 1.0 / e[r][r]
            o_ref[rows_of(8 * p + r), :] = rows[r] * lax.rsqrt(e[r][r])
            pivot = rows[r] * g
            scaled = [e[r][c] * g if c > r else None for c in range(8)]
            for s in range(8):
                if s == r:
                    continue
                f = e[r][s] if s > r else e[s][r]
                rows[s] = rows[s] - f * pivot
                for c in range(max(s, r + 1), 8):
                    e[s][c] = e[s][c] - f * scaled[c]
            rows[r] = pivot
            e[r] = scaled
        for i in range(8 * (p + 1), 8 * panels):
            row = s_ref[rows_of(i), :]
            total = row
            for r in range(8):
                total = total - spread(row, first + 8 * p + r) * rows[r]
            s_ref[rows_of(i), :] = total


def iterate_kernel(inv_rows, b_ref, start_ref, coef_ref, pb_ref,
                   gh, gl, yh, yl, ah, al, th, tl, wh, wl, s_ref, o_ref):
    for n, (i, j) in enumerate(PAIRS):
        block = b_ref[n % 2, n // 2]
        hi, lo = split(block)
        gh[pl.ds(256 * i, 256), pl.ds(256 * j, 256)] = hi
        gl[pl.ds(256 * i, 256), pl.ds(256 * j, 256)] = lo
        if i != j:
            hi, lo = split(block.T)
            gh[pl.ds(256 * j, 256), pl.ds(256 * i, 256)] = hi
            gl[pl.ds(256 * j, 256), pl.ds(256 * i, 256)] = lo

    def times_gram(hi, lo):
        return dot(hi, gh[...], NN) + (dot(hi, gl[...], NN) + dot(lo, gh[...], NN))

    shi, slo = split(start_ref[...])
    first = split(times_gram(shi, slo))
    yh[0], yl[0] = first
    ah[0], al[0] = first
    th[...] = jnp.zeros_like(th)
    tl[...] = jnp.zeros_like(tl)
    s_ref[...] = jnp.ones_like(s_ref)

    row = lax.broadcasted_iota(jnp.int32, (NB, 256), 0)
    lane = lax.broadcasted_iota(jnp.int32, (NB, 256), 1)
    row2, lane2 = row[:, :128], lane[:, :128]

    def step(t, carry):
        vaug = []
        for j in range(NJ):
            k = t - j
            valid = (k >= 0) & (k <= 4)
            kr = jnp.clip(k, 0, 4)
            here = pl.ds(NB * j, NB)
            a = (ah[kr, here, :], al[kr, here, :])
            y = (yh[kr, here, :], yl[kr, here, :])
            scale = jnp.where(k == 4, inv_rows, 1.0).astype(F32)
            twice = tuple(jnp.concatenate([v, v], axis=0) for v in y)
            d = dot3(a, twice, NT) * scale
            w = a[0].astype(F32) + a[1].astype(F32)
            v = (lane == row + NB * j).astype(F32)
            if j > 0:
                before = pl.ds(0, NB * j)
                m = dot3(a, (yh[kr, before, :], yl[kr, before, :]), NT) * scale
                tri = (th[kr, before, before], tl[kr, before, before])
                low = split(dot3(split(m), tri, NT))
                low2 = tuple(jnp.concatenate([x, x], axis=0) for x in low)
                d = d - dot3(low, low2, NT)
                wide = (th[kr, before, :], tl[kr, before, :])
                coef = dot3(low, wide, NN)
                v = v - coef
                ch, cl = split(coef[:, :NB * j])
                w = w - dot3((ch, cl), (ah[kr, before, :], al[kr, before, :]), NN)
            vaug.append(v)
            wh[here, :], wl[here, :] = split(w)
            eye = (row2 == lane2)
            d = jnp.where(valid, d, (lane2 == row2 + NB).astype(F32))
            s_ref[pl.ds(j, NB, stride=8), :] = jnp.where(lane2 < NB, eye.astype(F32), d)
        z = times_gram(wh[...], wl[...])
        inverse_factors(s_ref, o_ref, 8, NB)
        for j in range(NJ):
            k = t - j
            valid = (k >= 0) & (k <= 4)
            kw = jnp.where(valid, k, 5)
            kn = jnp.where(valid, k + 1, 6)
            here = pl.ds(NB * j, NB)
            inv = split(o_ref[pl.ds(j, NB, stride=8), :][:, :NB])
            th[kw, here, :], tl[kw, here, :] = split(dot3(inv, split(vaug[j]), NN))
            y = split(dot3(inv, split(z[NB * j:NB * (j + 1), :]), NN))
            q = dot3(inv, (wh[here, :], wl[here, :]), NN)
            yh[kn, here, :], yl[kn, here, :] = y
            last = k >= 3
            qh, ql = split(q)
            ah[kn, here, :] = jnp.where(last, qh, y[0])
            al[kn, here, :] = jnp.where(last, ql, y[1])
        return carry

    lax.fori_loop(0, 8, step, 0)
    coef = ah[5]
    coef_ref[...] = coef

    for part in range(4):
        xs = b_ref[0, 5, pl.ds(32 * part, 32), :].astype(BF16)
        term = dot(xs, coef[:, 256 * part:256 * (part + 1)], NT)
        panel = term if part == 0 else panel + term
    ph = split(panel)
    twice = tuple(jnp.concatenate([x, x, x, x], axis=0) for x in ph)
    d = dot3(ph, twice, NT)
    r3 = lax.broadcasted_iota(jnp.int32, (32, 128), 0)
    l3 = lax.broadcasted_iota(jnp.int32, (32, 128), 1)
    s_ref[...] = jnp.ones_like(s_ref)
    s_ref[pl.ds(0, 32, stride=8), :] = jnp.where(l3 < 32, (l3 == r3).astype(F32), d)
    inverse_factors(s_ref, o_ref, 4, 32)
    inv = split(o_ref[pl.ds(0, 32, stride=8), :][:, :32])
    pb_ref[...] = dot3(inv, ph, NN).T


def iterate_call(packed, start_t, inv_rows):
    return pl.pallas_call(
        functools.partial(iterate_kernel, inv_rows),
        out_shape=(jax.ShapeDtypeStruct((256, 1024), BF16), jax.ShapeDtypeStruct((256, 32), F32)),
        in_specs=[pl.BlockSpec(memory_space=pltpu.VMEM)] * 2,
        out_specs=(pl.BlockSpec(memory_space=pltpu.VMEM),) * 2,
        scratch_shapes=[
            pltpu.VMEM((1024, 1024), BF16), pltpu.VMEM((1024, 1024), BF16),
            pltpu.VMEM((7, 256, 1024), BF16), pltpu.VMEM((7, 256, 1024), BF16),
            pltpu.VMEM((7, 256, 1024), BF16), pltpu.VMEM((7, 256, 1024), BF16),
            pltpu.VMEM((6, 256, 256), BF16), pltpu.VMEM((6, 256, 256), BF16),
            pltpu.VMEM((256, 1024), BF16), pltpu.VMEM((256, 1024), BF16),
            pltpu.VMEM((512, 128), F32), pltpu.VMEM((512, 128), F32),
        ],
        compiler_params=pltpu.CompilerParams(vmem_limit_bytes=56 * 1024 * 1024),
        name="iterate",
    )(packed, start_t)


def project_kernel(x_ref, coef_ref, pb_ref, modes_ref, scores_ref, proj_hi, proj_lo):
    @pl.when(pl.program_id(0) == 0)
    def _():
        pb = split(pb_ref[...])
        proj_hi[...], proj_lo[...] = split(dot3(pb, pb, NT))

    basis = dot(x_ref[...], coef_ref[...], NT)
    hi, lo = split(basis)
    modes_ref[...] = hi
    remaining = basis - dot3((hi, lo), (proj_hi[...], proj_lo[...]), NN)
    hi, lo = split(remaining * remaining)
    ones = jnp.ones((8, hi.shape[1]), BF16)
    total = dot(ones, hi, NT) + dot(ones, lo, NT)
    scores_ref[0] = total[:1] * (1.0 / hi.shape[1])


def project_call(x, coef_t, pb):
    rows = 256
    steps = x.shape[0] // rows
    return pl.pallas_call(
        project_kernel,
        grid=(steps,),
        out_shape=(jax.ShapeDtypeStruct((x.shape[0], 256), BF16), jax.ShapeDtypeStruct((steps, 1, rows), F32)),
        in_specs=[pl.BlockSpec((rows, 1024), lambda i: (i, 0)), pl.BlockSpec((256, 1024), lambda i: (0, 0)),
                  pl.BlockSpec((256, 32), lambda i: (0, 0))],
        out_specs=(pl.BlockSpec((rows, 256), lambda i: (i, 0)), pl.BlockSpec((1, 1, rows), lambda i: (i, 0, 0))),
        scratch_shapes=[pltpu.VMEM((256, 256), BF16), pltpu.VMEM((256, 256), BF16)],
        compiler_params=pltpu.CompilerParams(vmem_limit_bytes=32 * 1024 * 1024),
        name="project",
    )(x, coef_t, pb)


def local(snapshots, start, pivot_dev, pivot_row):
    rows_total = snapshots.shape[0] * lax.axis_size(AXES)
    packed = reduce_call(snapshots, pivot_dev[:, None], pivot_row[:, None])
    coef_t, panel_basis = iterate_call(packed.reshape(2, 6, 256, 256), start.T, 1.0 / rows_total)
    modes, scores = project_call(snapshots, coef_t, panel_basis)
    return (modes, scores.reshape(-1), panel_basis)


def solution(mesh):
    torus = Mesh(mesh.devices.reshape(4, 4, 4, 2), AXES)
    rows = ("y", "core", "x", "z")
    return jax.shard_map(
        local,
        mesh=torus,
        in_specs=(P(rows, None), P(), P(), P()),
        out_specs=(P(rows, None), P(rows), P()),
        check_vma=False,
    )
```

time: 625 us -> 146 us (0.23); the launches traced: 614 us -> 146 us
  other arithmetic: 279 us -> 0 us
  waiting for transfers between devices: 157 us -> 0 us
  Pallas kernels: 0 us -> 134 us
  matrix products: 70.2 us -> 0 us
  blocking collectives: 44.8 us -> 0 us
  between operations: 34.5 us -> 0.65 us
  local copies, waits for them, and re-layouts: 27.6 us -> 11.4 us
    another operation x50 -> x0, other arithmetic: 278 us -> none  [the longest x27 138 us: local(): iterate = right_solve(jnp.linalg.cholesky(square), image)]
    psum x1 -> x0, waiting for transfers between devices: 157 us -> none  [local(): gram_full = lax.psum(local_gram, GRP_BLK)]
    pallas_call x0 -> x3, Pallas kernels: none -> 134 us  [the longest x1 76.5 us: iterate_call(): pl.pallas_call(functools.partial(iterate_kernel, inv_rows), out_shape=(ja...]
    dot_general x15 -> x0, matrix products: 56.7 us -> none  [the longest x5 27.4 us: apply_gram(): return jnp.dot(gram_full, iterate, precision=lax.Precision.HIGHEST)]
    psum x4 -> x0, blocking collectives: 44.8 us -> none  [over_axes(): array = lax.psum(array, axis)]
    another operation x46 -> x0, local copies, waits for them, and re-layouts: 19.9 us -> none  [the longest x36 19.8 us: right_solve(): lax.linalg.triangular_solve(factor, matrix, left_side=False, lower=True,...]
    another operation x26 -> x0, matrix products: 13.5 us -> none  [the longest x16 11.1 us: right_solve(): lax.linalg.triangular_solve(factor, matrix, left_side=False, lower=True,...]
    unnamed x9 -> x10, local copies, waits for them, and re-layouts: 2.89 us -> 9.9 us
  transfers between devices with their start and end apart: 1 -> 0, of which waited for: 1 -> 0; matrix products, arithmetic and copies ran while one was open for 0% -> 0% of each run, Pallas kernels for 0% -> 0%
where the time goes in v1:
time: 146 us
  Pallas kernels  134 us (92%)
  local copies, waits for them, and re-layouts  11.4 us (8%)
    pallas_call x1, Pallas kernels, iterate_call(): pl.pallas_call(functools.partial(iterate_kernel, inv_rows), out_shape=(ja...  76.5 us
    pallas_call x1, Pallas kernels, reduce_call(): pl.pallas_call(reduce_kernel, out_shape=jax.ShapeDtypeStruct((2, 3, 4, 4,...  48.9 us
    unnamed x10, local copies, waits for them, and re-layouts  9.9 us
    pallas_call x1, Pallas kernels, project_call(): pl.pallas_call(project_kernel, grid=(steps,), out_shape=(jax.ShapeDtypeSt...  8.11 us

profile of v1, /device:TPU:1, one launch (start us, length us, event | category | flops | bytes accessed | tf_op | source)
XLA Modules:
  0.0 145.6 jit_solution(17546669417709592877)
XLA Ops:
  0.6 0.7 copy.7.pdev_ref
  1.4 0.7 copy.8.prow_ref
  2.1 2.5 %copy.9 = f32[1024,256]{0,1:T(8,128)} copy(f32[1024,256]{1,0:T(8,128)} %param.5) | data formatting | bytes 2097152 | tf_op args[1]
  4.6 48.9 %gram_sum.1 = f32[2,3,4,4,4,8,256]{6,5,4,3,2,1,0:T(8,128)S(1)} custom-call(bf16[2048,1024]{1,0:T(8,128)(2,1)} %x_ref.3, s32[32,1]{1,0:T(8,128)S(1)} %copy.7.pdev_ref, s32[32,1]{1,0:T(8,128)S(1)} %copy.8.prow_ref), custom_call_target="tpu_custom_call" | custom-call | tf_op jit(solution)/shard_map/gram_sum/pallas_call | solution.py:166
  53.6 0.0 copy-start.1
  53.6 1.6 %copy-done.1 = f32[2,3,4,4,4,8,256]{6,5,4,3,2,1,0:T(8,128)} copy-done((f32[2,3,4,4,4,8,256]{6,5,4,3,2,1,0:T(8,128)}, f32[2,3,4,4,4,8,256]{6,5,4,3,2,1,0:T(8,128)S(1)}, u32[]{:S(2)}) %copy-start.1) | copy-done | bytes 3145752
  55.2 76.5 %iterate.1 = (bf16[256,1024]{1,0:T(8,128)(2,1)}, f32[256,32]{1,0:T(8,128)}) custom-call(f32[2,6,256,256]{3,2,1,0:T(8,128)} %bitcast.5, f32[256,1024]{1,0:T(8,128)} %bitcast.6), custom_call_target="tpu_custom_call" | custom-call | tf_op jit(solution)/shard_map/iterate/pallas_call | solution.py:311
  131.8 1.6 %copy.10 = f32[256,32]{0,1:T(8,128)} copy(f32[256,32]{1,0:T(8,128)} %get-tuple-element.13.pb_ref) | data formatting | bytes 65536
  133.4 0.0 copy-start
  133.4 2.2 %copy-done = bf16[2048,1024]{1,0:T(8,128)(2,1)S(1)} copy-done((bf16[2048,1024]{1,0:T(8,128)(2,1)S(1)}, bf16[2048,1024]{1,0:T(8,128)(2,1)}, u32[]{:S(2)}) %copy-start) | copy-done | bytes 4194328
  135.6 0.0 copy-start.2
  135.6 1.0 copy-done.2
  136.6 0.0 copy-start.3
  136.6 0.9 copy-done.3
  137.5 8.1 %project.1 = (bf16[2048,256]{1,0:T(8,128)(2,1)}, f32[8,1,256]{2,1,0:T(1,128)}) custom-call(bf16[2048,1024]{1,0:T(8,128)(2,1)S(1)} %copy-done, bf16[256,1024]{1,0:T(8,128)(2,1)S(1)} %copy-done.2, f32[256,32]{1,0:T(8,128)S(1)} %copy-done.3), custom_call_target="tpu_custom_call" | custom-call | tf_op jit(solution)/shard_map/project/pallas_call | solution.py:348
Async XLA Ops:
  53.6 1.7 %copy-start.1 = (f32[2,3,4,4,4,8,256]{6,5,4,3,2,1,0:T(8,128)}, f32[2,3,4,4,4,8,256]{6,5,4,3,2,1,0:T(8,128)S(1)}, u32[]{:S(2)}) copy-start(f32[2,3,4,4,4,8,256]{6,5,4,3,2,1,0:T(8,128)S(1)} %gram_sum.1) | copy-start | bytes 9437188
  133.4 2.2 %copy-start = (bf16[2048,1024]{1,0:T(8,128)(2,1)S(1)}, bf16[2048,1024]{1,0:T(8,128)(2,1)}, u32[]{:S(2)}) copy-start(bf16[2048,1024]{1,0:T(8,128)(2,1)} %x_ref.3) | copy-start | bytes 12582916
  135.6 1.0 copy-start.2
  136.6 0.9 copy-start.3

commit v2 on v1

--- a/solution.py
+++ b/solution.py
@@ -182,36 +182,68 @@
     )(x, pdev, prow)
 
 
-def inverse_factors(s_ref, o_ref, panels, first):
-    rows_of = lambda i: pl.ds(8 * i, 8)
-    spread = lambda row, c: jnp.broadcast_to(row[:, c:c + 1], (8, 128))
+def inverse_factors(augs, panels, first, work=()):
+    sub = lax.broadcasted_iota(jnp.int32, (8, 128), 0)
+    spread = lambda v, c: jnp.broadcast_to(v[:, c:c + 1], (8, 128))
+    one = lambda v, r: jnp.broadcast_to(v[r:r + 1, :], (8, 128))
+    every = range(len(augs))
+    work, done = list(work), 0
+    groups = [[aug[8 * q:8 * q + 8, :] for q in range(panels)] for aug in augs]
+    outs = [[] for _ in every]
+    late = []
+
+    def columns_of(n, q, p):
+        return [spread(groups[n][q], first + 8 * p + c) for c in range(8)]
+
+    def reduce(n, q, columns, lines):
+        terms = [columns[r] * lines[r] for r in range(8)]
+        while len(terms) > 1:
+            terms = [terms[i] + terms[i + 1] for i in range(0, len(terms), 2)]
+        groups[n][q] = groups[n][q] - terms[0]
+
     for p in range(panels):
-        rows = [s_ref[rows_of(8 * p + r), :] for r in range(8)]
-        e = [[spread(rows[r], first + 8 * p + c) if c >= r else None for c in range(8)] for r in range(8)]
+        v = [groups[n][p] for n in every]
+        out = list(v)
+        columns = [columns_of(n, p, p) for n in every]
+        below = {}
         for r in range(8):
-            g = 1.0 / e[r][r]
-            o_ref[rows_of(8 * p + r), :] = rows[r] * lax.rsqrt(e[r][r])
-            pivot = rows[r] * g
-            scaled = [e[r][c] * g if c > r else None for c in range(8)]
-            for s in range(8):
-                if s == r:
-                    continue
-                f = e[r][s] if s > r else e[s][r]
-                rows[s] = rows[s] - f * pivot
-                for c in range(max(s, r + 1), 8):
-                    e[s][c] = e[s][c] - f * scaled[c]
-            rows[r] = pivot
-            e[r] = scaled
-        for i in range(8 * (p + 1), 8 * panels):
-            row = s_ref[rows_of(i), :]
-            total = row
-            for r in range(8):
-                total = total - spread(row, first + 8 * p + r) * rows[r]
-            s_ref[rows_of(i), :] = total
-
-
-def iterate_kernel(inv_rows, b_ref, start_ref, coef_ref, pb_ref,
-                   gh, gl, yh, yl, ah, al, th, tl, wh, wl, s_ref, o_ref):
+            for n in every:
+                here = columns[n][r]
+                pivot = one(here, r)
+                inverse = 1.0 / pivot
+                line = one(v[n], r)
+                for c in range(r + 1, 8):
+                    value = one(columns[n][c], r) * inverse
+                    columns[n][c] = jnp.where(sub == r, value, columns[n][c] - here * value)
+                out[n] = jnp.where(sub == r, line * lax.rsqrt(pivot), out[n])
+                line = line * inverse
+                v[n] = jnp.where(sub == r, line, v[n] - here * line)
+            share = -(-len(late) // max(1, 6 - r))
+            for n, q, lines in late[:share]:
+                reduce(n, q, columns_of(n, q, p - 1), lines)
+            late = late[share:]
+            if r == 5 and p + 1 < panels:
+                assert not late
+                below = {n: columns_of(n, p + 1, p) for n in every}
+            target = len(work) * (8 * p + r + 1) // (8 * panels)
+            while done < target:
+                work[done]()
+                done += 1
+        for n in every:
+            outs[n].append(out[n])
+            lines = [one(v[n], r) for r in range(8)]
+            if p + 1 < panels:
+                reduce(n, p + 1, below[n], lines)
+            late += [(n, q, lines) for q in range(p + 2, panels)]
+        late.sort(key=lambda item: item[1])
+    return [jnp.concatenate(o, axis=0) for o in outs]
+
+
+def iterate_kernel(inv_rows, b_ref, start_ref, x_hbm, modes_hbm, scores_ref, pb_ref,
+                   gh, gl, sh, sl, yh, yl, qh, ql, th, tl, wh, wl, zh, zl, zf, x_ref, modes_ref, basis_ref,
+                   x_sem, modes_sem):
+    load = pltpu.make_async_copy(x_hbm, x_ref, x_sem)
+    load.start()
     for n, (i, j) in enumerate(PAIRS):
         block = b_ref[n % 2, n // 2]
         hi, lo = split(block)
@@ -221,148 +253,169 @@
             hi, lo = split(block.T)
             gh[pl.ds(256 * j, 256), pl.ds(256 * i, 256)] = hi
             gl[pl.ds(256 * j, 256), pl.ds(256 * i, 256)] = lo
+    sh[...], sl[...] = split(start_ref[...].T)
 
     def times_gram(hi, lo):
         return dot(hi, gh[...], NN) + (dot(hi, gl[...], NN) + dot(lo, gh[...], NN))
 
-    shi, slo = split(start_ref[...])
-    first = split(times_gram(shi, slo))
-    yh[0], yl[0] = first
-    ah[0], al[0] = first
+    def block(j):
+        return pl.ds(NB * j, NB)
+
+    yh[0, block(0), :], yl[0, block(0), :] = split(times_gram(sh[block(0), :], sl[block(0), :]))
     th[...] = jnp.zeros_like(th)
     tl[...] = jnp.zeros_like(tl)
-    s_ref[...] = jnp.ones_like(s_ref)
 
     row = lax.broadcasted_iota(jnp.int32, (NB, 256), 0)
     lane = lax.broadcasted_iota(jnp.int32, (NB, 256), 1)
-    row2, lane2 = row[:, :128], lane[:, :128]
-
-    def step(t, carry):
-        vaug = []
-        for j in range(NJ):
-            k = t - j
-            valid = (k >= 0) & (k <= 4)
-            kr = jnp.clip(k, 0, 4)
-            here = pl.ds(NB * j, NB)
-            a = (ah[kr, here, :], al[kr, here, :])
-            y = (yh[kr, here, :], yl[kr, here, :])
-            scale = jnp.where(k == 4, inv_rows, 1.0).astype(F32)
-            twice = tuple(jnp.concatenate([v, v], axis=0) for v in y)
-            d = dot3(a, twice, NT) * scale
-            w = a[0].astype(F32) + a[1].astype(F32)
+    eye = (row == lane)[:, :NB].astype(F32)
+
+    def stacked3(a, b, dims):
+        n = a[0].shape[0]
+        both = dot(jnp.concatenate([a[0], a[1]], axis=0), b[0], dims)
+        return both[:n] + both[n:] + dot(a[0], b[1], dims)
+
+    for t in range(8):
+        tasks = [(t - j, j) for j in range(NJ) if 0 <= t - j <= 4]
+        go = [(k, j) for k, j in tasks if k < 4]
+        ahead = t < 3
+        ms, ds, lows, vaug, coefs, part = {}, {}, {}, {}, {}, {}
+
+        def left(k, where, lanes=slice(None)):
+            return (yh[k, where, lanes], yl[k, where, lanes]) if k < 4 else (qh[where, lanes], ql[where, lanes])
+
+        for k, j in tasks:
+            scale = inv_rows if k == 4 else 1.0
+            a = left(k, block(j))
+            ds[k] = stacked3(a, (yh[k, block(j), :], yl[k, block(j), :]), NT) * scale
+            if j > 0:
+                before = pl.ds(0, NB * j)
+                ms[k] = split(stacked3(a, (yh[k, before, :], yl[k, before, :]), NT) * scale)
+        for k, j in tasks:
+            if j > 0:
+                before = pl.ds(0, NB * j)
+                lows[k] = split(stacked3(ms[k], (th[k, before, before], tl[k, before, before]), NT))
+        for k, j in tasks:
+            if j > 0:
+                ds[k] = ds[k] - stacked3(lows[k], lows[k], NT)
+
+        def make_v(k, j):
             v = (lane == row + NB * j).astype(F32)
             if j > 0:
-                before = pl.ds(0, NB * j)
-                m = dot3(a, (yh[kr, before, :], yl[kr, before, :]), NT) * scale
-                tri = (th[kr, before, before], tl[kr, before, before])
-                low = split(dot3(split(m), tri, NT))
-                low2 = tuple(jnp.concatenate([x, x], axis=0) for x in low)
-                d = d - dot3(low, low2, NT)
-                wide = (th[kr, before, :], tl[kr, before, :])
-                coef = dot3(low, wide, NN)
+                coef = stacked3(lows[k], (th[k, pl.ds(0, NB * j), :], tl[k, pl.ds(0, NB * j), :]), NN)
                 v = v - coef
-                ch, cl = split(coef[:, :NB * j])
-                w = w - dot3((ch, cl), (ah[kr, before, :], al[kr, before, :]), NN)
-            vaug.append(v)
-            wh[here, :], wl[here, :] = split(w)
-            eye = (row2 == lane2)
-            d = jnp.where(valid, d, (lane2 == row2 + NB).astype(F32))
-            s_ref[pl.ds(j, NB, stride=8), :] = jnp.where(lane2 < NB, eye.astype(F32), d)
-        z = times_gram(wh[...], wl[...])
-        inverse_factors(s_ref, o_ref, 8, NB)
-        for j in range(NJ):
-            k = t - j
-            valid = (k >= 0) & (k <= 4)
-            kw = jnp.where(valid, k, 5)
-            kn = jnp.where(valid, k + 1, 6)
-            here = pl.ds(NB * j, NB)
-            inv = split(o_ref[pl.ds(j, NB, stride=8), :][:, :NB])
-            th[kw, here, :], tl[kw, here, :] = split(dot3(inv, split(vaug[j]), NN))
-            y = split(dot3(inv, split(z[NB * j:NB * (j + 1), :]), NN))
-            q = dot3(inv, (wh[here, :], wl[here, :]), NN)
-            yh[kn, here, :], yl[kn, here, :] = y
-            last = k >= 3
-            qh, ql = split(q)
-            ah[kn, here, :] = jnp.where(last, qh, y[0])
-            al[kn, here, :] = jnp.where(last, ql, y[1])
-        return carry
-
-    lax.fori_loop(0, 8, step, 0)
-    coef = ah[5]
-    coef_ref[...] = coef
-
+                coefs[k] = split(coef[:, :NB * j])
+            vaug[k] = split(v)
+
+        def make_w(n, k, j, lanes):
+            a = left(k, block(j), lanes)
+            if j > 0:
+                w = a[0].astype(F32) + a[1].astype(F32)
+                a = split(w - stacked3(coefs[k], left(k, pl.ds(0, NB * j), lanes), NN))
+            wh[block(n), lanes], wl[block(n), lanes] = a
+
+        def make_ahead():
+            n = len(go)
+            wh[block(n), :], wl[block(n), :] = sh[block(t + 1), :], sl[block(t + 1), :]
+
+        rows = NB * (len(go) + ahead)
+
+        def make_z(lanes, depth, last):
+            new = stacked3((wh[:rows, depth], wl[:rows, depth]), (gh[depth, lanes], gl[depth, lanes]), NN)
+            part[0] = new if depth.start == 0 else part[0] + new
+            if last:
+                zh[:rows, lanes], zl[:rows, lanes] = split(part[0])
+
+        work = [functools.partial(make_v, k, j) for k, j in tasks]
+        work += [functools.partial(make_w, n, k, j, slice(512 * i, 512 * i + 512))
+                 for n, (k, j) in enumerate(go + [task for task in tasks if task not in go]) for i in range(2)]
+        if ahead:
+            work.append(make_ahead)
+        if rows:
+            work += [functools.partial(make_z, slice(256 * i, 256 * i + 256), slice(256 * d, 256 * d + 256), d == 3)
+                     for i in range(4) for d in range(4)]
+        invs = inverse_factors([jnp.concatenate([eye, ds[k]], axis=1) for k, j in tasks], 8, NB, work)
+        invs = {k: split(inv[:, :NB]) for (k, j), inv in zip(tasks, invs)}
+        for n, (k, j) in enumerate(go):
+            yh[k + 1, block(j), :], yl[k + 1, block(j), :] = split(stacked3(invs[k], (zh[block(n), :], zl[block(n), :]), NN))
+            if k == 3:
+                qh[block(j), :], ql[block(j), :] = split(stacked3(invs[k], (wh[block(n), :], wl[block(n), :]), NN))
+        if ahead:
+            n = len(go)
+            yh[0, block(t + 1), :], yl[0, block(t + 1), :] = zh[block(n), :], zl[block(n), :]
+        for k, j in tasks:
+            if j < NJ - 1:
+                th[k, block(j), :], tl[k, block(j), :] = split(stacked3(invs[k], vaug[k], NN))
+            if k == 4:
+                n = len(go)
+                zf[block(j), :] = stacked3(invs[k], (wh[block(n), :], wl[block(n), :]), NN).astype(BF16)
+
+    coef = zf[...]
     for part in range(4):
         xs = b_ref[0, 5, pl.ds(32 * part, 32), :].astype(BF16)
         term = dot(xs, coef[:, 256 * part:256 * (part + 1)], NT)
         panel = term if part == 0 else panel + term
     ph = split(panel)
-    twice = tuple(jnp.concatenate([x, x, x, x], axis=0) for x in ph)
-    d = dot3(ph, twice, NT)
-    r3 = lax.broadcasted_iota(jnp.int32, (32, 128), 0)
-    l3 = lax.broadcasted_iota(jnp.int32, (32, 128), 1)
-    s_ref[...] = jnp.ones_like(s_ref)
-    s_ref[pl.ds(0, 32, stride=8), :] = jnp.where(l3 < 32, (l3 == r3).astype(F32), d)
-    inverse_factors(s_ref, o_ref, 4, 32)
-    inv = split(o_ref[pl.ds(0, 32, stride=8), :][:, :32])
-    pb_ref[...] = dot3(inv, ph, NN).T
-
-
-def iterate_call(packed, start_t, inv_rows):
+    small = jnp.concatenate(
+        [eye[:32, :32], dot3(ph, ph, NT), jnp.zeros((32, 64), F32)], axis=1)
+
+    load.wait()
+    stores = []
+    for n in range(8):
+        here = pl.ds(256 * n, 256)
+        basis = dot(x_ref[here, :], coef, NT)
+        basis_ref[here, :] = basis
+        modes_ref[here, :] = basis.astype(BF16)
+        stores.append(pltpu.make_async_copy(modes_ref.at[here, :], modes_hbm.at[here, :], modes_sem.at[n]))
+        stores[-1].start()
+
+    inv = split(inverse_factors([small], 4, 32)[0][:, :32])
+    pbt = dot3(inv, ph, NN)
+    pb_ref[...] = pbt.T
+    pb = split(pbt.T)
+    proj = split(dot3(pb, pb, NT))
+    ones = jnp.ones((8, 256), BF16)
+    for n in range(8):
+        here = pl.ds(256 * n, 256)
+        basis = basis_ref[here, :]
+        remaining = basis - dot3(split(basis), proj, NN)
+        hi, lo = split(remaining * remaining)
+        total = dot(ones, hi, NT) + dot(ones, lo, NT)
+        scores_ref[n:n + 1, :] = total[:1] * (1.0 / 256)
+    for copy in stores:
+        copy.wait()
+
+
+def iterate_call(packed, start, x, inv_rows):
+    vmem = lambda: pl.BlockSpec(memory_space=pltpu.VMEM)
+    hbm = lambda: pl.BlockSpec(memory_space=pltpu.HBM)
+    rows = x.shape[0]
     return pl.pallas_call(
         functools.partial(iterate_kernel, inv_rows),
-        out_shape=(jax.ShapeDtypeStruct((256, 1024), BF16), jax.ShapeDtypeStruct((256, 32), F32)),
-        in_specs=[pl.BlockSpec(memory_space=pltpu.VMEM)] * 2,
-        out_specs=(pl.BlockSpec(memory_space=pltpu.VMEM),) * 2,
+        out_shape=(jax.ShapeDtypeStruct((rows, 256), BF16), jax.ShapeDtypeStruct((8, 256), F32),
+                   jax.ShapeDtypeStruct((256, 32), F32)),
+        in_specs=[vmem(), vmem(), hbm()],
+        out_specs=(hbm(), vmem(), vmem()),
         scratch_shapes=[
             pltpu.VMEM((1024, 1024), BF16), pltpu.VMEM((1024, 1024), BF16),
-            pltpu.VMEM((7, 256, 1024), BF16), pltpu.VMEM((7, 256, 1024), BF16),
-            pltpu.VMEM((7, 256, 1024), BF16), pltpu.VMEM((7, 256, 1024), BF16),
-            pltpu.VMEM((6, 256, 256), BF16), pltpu.VMEM((6, 256, 256), BF16),
             pltpu.VMEM((256, 1024), BF16), pltpu.VMEM((256, 1024), BF16),
-            pltpu.VMEM((512, 128), F32), pltpu.VMEM((512, 128), F32),
+            pltpu.VMEM((5, 256, 1024), BF16), pltpu.VMEM((5, 256, 1024), BF16),
+            pltpu.VMEM((256, 1024), BF16), pltpu.VMEM((256, 1024), BF16),
+            pltpu.VMEM((5, 256, 256), BF16), pltpu.VMEM((5, 256, 256), BF16),
+            pltpu.VMEM((256, 1024), BF16), pltpu.VMEM((256, 1024), BF16),
+            pltpu.VMEM((256, 1024), BF16), pltpu.VMEM((256, 1024), BF16),
+            pltpu.VMEM((256, 1024), BF16),
+            pltpu.VMEM((rows, 1024), BF16), pltpu.VMEM((rows, 256), BF16), pltpu.VMEM((rows, 256), F32),
+            pltpu.SemaphoreType.DMA, pltpu.SemaphoreType.DMA((8,)),
         ],
         compiler_params=pltpu.CompilerParams(vmem_limit_bytes=56 * 1024 * 1024),
         name="iterate",
-    )(packed, start_t)
-
-
-def project_kernel(x_ref, coef_ref, pb_ref, modes_ref, scores_ref, proj_hi, proj_lo):
-    @pl.when(pl.program_id(0) == 0)
-    def _():
-        pb = split(pb_ref[...])
-        proj_hi[...], proj_lo[...] = split(dot3(pb, pb, NT))
-
-    basis = dot(x_ref[...], coef_ref[...], NT)
-    hi, lo = split(basis)
-    modes_ref[...] = hi
-    remaining = basis - dot3((hi, lo), (proj_hi[...], proj_lo[...]), NN)
-    hi, lo = split(remaining * remaining)
-    ones = jnp.ones((8, hi.shape[1]), BF16)
-    total = dot(ones, hi, NT) + dot(ones, lo, NT)
-    scores_ref[0] = total[:1] * (1.0 / hi.shape[1])
-
-
-def project_call(x, coef_t, pb):
-    rows = 256
-    steps = x.shape[0] // rows
-    return pl.pallas_call(
-        project_kernel,
-        grid=(steps,),
-        out_shape=(jax.ShapeDtypeStruct((x.shape[0], 256), BF16), jax.ShapeDtypeStruct((steps, 1, rows), F32)),
-        in_specs=[pl.BlockSpec((rows, 1024), lambda i: (i, 0)), pl.BlockSpec((256, 1024), lambda i: (0, 0)),
-                  pl.BlockSpec((256, 32), lambda i: (0, 0))],
-        out_specs=(pl.BlockSpec((rows, 256), lambda i: (i, 0)), pl.BlockSpec((1, 1, rows), lambda i: (i, 0, 0))),
-        scratch_shapes=[pltpu.VMEM((256, 256), BF16), pltpu.VMEM((256, 256), BF16)],
-        compiler_params=pltpu.CompilerParams(vmem_limit_bytes=32 * 1024 * 1024),
-        name="project",
-    )(x, coef_t, pb)
+    )(packed, start, x)
 
 
 def local(snapshots, start, pivot_dev, pivot_row):
     rows_total = snapshots.shape[0] * lax.axis_size(AXES)
     packed = reduce_call(snapshots, pivot_dev[:, None], pivot_row[:, None])
-    coef_t, panel_basis = iterate_call(packed.reshape(2, 6, 256, 256), start.T, 1.0 / rows_total)
-    modes, scores = project_call(snapshots, coef_t, panel_basis)
+    modes, scores, panel_basis = iterate_call(packed.reshape(2, 6, 256, 256), start, snapshots, 1.0 / rows_total)
     return (modes, scores.reshape(-1), panel_basis)
 
 

time: 146 us -> 99.8 us (0.68)
  Pallas kernels: 134 us -> 92.9 us
  local copies, waits for them, and re-layouts: 11.4 us -> 6.02 us
    pallas_call x1, Pallas kernels: 76.5 us -> 43.9 us  [iterate_call(): pl.pallas_call(functools.partial(iterate_kernel, inv_rows), out_shape=(ja...]
    pallas_call x1 -> x0, Pallas kernels: 8.11 us -> none  [project_call(): pl.pallas_call(project_kernel, grid=(steps,), out_shape=(jax.ShapeDtypeSt...]
    unnamed x10 -> x4, local copies, waits for them, and re-layouts: 9.9 us -> 4.54 us
where the time goes in v2:
time: 99.8 us; the launch traced here: 99.5 us
  Pallas kernels  92.9 us (93%)
  local copies, waits for them, and re-layouts  6.02 us (6%)
    pallas_call x1, Pallas kernels, reduce_call(): pl.pallas_call(reduce_kernel, out_shape=jax.ShapeDtypeStruct((2, 3, 4, 4,...  48.9 us
    pallas_call x1, Pallas kernels, iterate_call(): pl.pallas_call(functools.partial(iterate_kernel, inv_rows), out_shape=(ja...  43.9 us
    unnamed x4, local copies, waits for them, and re-layouts  4.54 us

profile of v2, /device:TPU:1, one launch (start us, length us, event | category | flops | bytes accessed | tf_op | source)
XLA Modules:
  0.0 99.5 jit_solution(245039100906202775)
XLA Ops:
  0.6 0.7 copy.7.pdev_ref
  1.4 0.7 copy.8.prow_ref
  2.1 48.9 %gram_sum.1 = f32[2,3,4,4,4,8,256]{6,5,4,3,2,1,0:T(8,128)S(1)} custom-call(bf16[2048,1024]{1,0:T(8,128)(2,1)} %x_hbm.1, s32[32,1]{1,0:T(8,128)S(1)} %copy.7.pdev_ref, s32[32,1]{1,0:T(8,128)S(1)} %copy.8.prow_ref), custom_call_target="tpu_custom_call" | custom-call | tf_op jit(solution)/shard_map/gram_sum/pallas_call | solution.py:166
  51.1 0.0 copy-start
  51.1 1.6 %copy-done = f32[2,3,4,4,4,8,256]{6,5,4,3,2,1,0:T(8,128)} copy-done((f32[2,3,4,4,4,8,256]{6,5,4,3,2,1,0:T(8,128)}, f32[2,3,4,4,4,8,256]{6,5,4,3,2,1,0:T(8,128)S(1)}, u32[]{:S(2)}) %copy-start) | copy-done | bytes 3145752
  52.7 43.9 %iterate.1 = (bf16[2048,256]{1,0:T(8,128)(2,1)}, f32[8,256]{1,0:T(8,128)}, f32[256,32]{1,0:T(8,128)}) custom-call(f32[2,6,256,256]{3,2,1,0:T(8,128)} %bitcast.5, f32[1024,256]{1,0:T(8,128)} %start_ref.1, bf16[2048,1024]{1,0:T(8,128)(2,1)} %x_hbm.1), custom_call_target="tpu_custom_call" | custom-call | tf_op jit(solution)/shard_map/iterate/pallas_call | solution.py:392
  96.6 1.3 %copy.10 = f32[1,2,8,128]{3,1,2,0:T(2,128)} copy(f32[1,2,8,128]{3,2,1,0:T(8,128)} %bitcast.7) | data formatting | bytes 16384
  97.9 1.6 %copy.9 = f32[256,32]{0,1:T(8,128)} copy(f32[256,32]{1,0:T(8,128)} %get-tuple-element.11) | data formatting | bytes 65536
Async XLA Ops:
  51.1 1.7 %copy-start = (f32[2,3,4,4,4,8,256]{6,5,4,3,2,1,0:T(8,128)}, f32[2,3,4,4,4,8,256]{6,5,4,3,2,1,0:T(8,128)S(1)}, u32[]{:S(2)}) copy-start(f32[2,3,4,4,4,8,256]{6,5,4,3,2,1,0:T(8,128)S(1)} %gram_sum.1) | copy-start | bytes 9437188

commit v3 on v2

--- a/solution.py
+++ b/solution.py
@@ -33,151 +33,162 @@
 TURNS = (("x", "y", "z"), ("y", "z", "x"), ("z", "x", "y"))
 
 
-def reduce_kernel(x_ref, pdev_ref, prow_ref, out_ref, loc, r0, acc, r1, a1, r2, a2, r3,
-                  send0, recv0, send_down, recv_down, send_up, recv_up, send4, recv4):
+def reduce_kernel(x_hbm, pdev_ref, prow_ref, out_ref, x_ref, loc, r0, acc, r1, a1, r2, x_sem,
+                  send0, recv0, send1, recv1, send2, recv2, send3, recv3, send4, recv4, send5, recv5):
     at = {name: lax.axis_index(name) for name in AXES}
     core = at["core"]
     other = 1 - core
 
+    slabs = [pltpu.make_async_copy(x_hbm.at[:, pl.ds(256 * i, 256)], x_ref.at[:, pl.ds(256 * i, 256)], x_sem.at[i])
+             for i in range(4)]
+    for slab in slabs:
+        slab.start()
+
+    def axis_peers(axis):
+        return [(d - 1, {axis: lax.rem(at[axis] + d, 4)}) for d in (1, 2, 3)]
+
+    def plane_peers(m):
+        one, two = TURNS[m % 3][1:]
+        return [(4 * d + e - 1, {one: lax.rem(at[one] + d, 4), two: lax.rem(at[two] + e, 4)})
+                for d in range(4) for e in range(4) if d or e]
+
     barrier = pltpu.get_barrier_semaphore()
     pl.semaphore_signal(barrier, inc=1, device_id={"core": other}, device_id_type=MESH)
     for axis in ("x", "y", "z"):
-        for d in (1, 2, 3):
-            pl.semaphore_signal(barrier, inc=1, device_id={axis: lax.rem(at[axis] + d, 4)}, device_id_type=MESH)
-    pl.semaphore_wait(barrier, 10)
-
-    def remote(src, dst, send, recv, axis, position):
-        return pltpu.make_async_remote_copy(src_ref=src, dst_ref=dst, send_sem=send, recv_sem=recv,
-                                            device_id={axis: position}, device_id_type=MESH)
+        for _, peer in axis_peers(axis):
+            pl.semaphore_signal(barrier, inc=1, device_id=peer, device_id_type=MESH)
+    for c in range(3):
+        for slot, peer in plane_peers(c):
+            if (slot + 1) // 4 and (slot + 1) % 4:
+                pl.semaphore_signal(barrier, inc=1, device_id=peer, device_id_type=MESH)
 
     sent = []
 
-    def go(copy):
+    def go(src, dst, send, recv, peer):
+        copy = pltpu.make_async_remote_copy(src_ref=src, dst_ref=dst, send_sem=send, recv_sem=recv,
+                                            device_id=peer, device_id_type=MESH)
         copy.start()
         sent.append(copy)
         return copy
 
-    swaps = {}
+    def keep(m, half, value):
+        loc[m, half, 0] = value[:, :128]
+        loc[m, half, 1] = value[:, 128:]
 
     def pair(m):
         for half in (0, 1):
             n = 2 * m + half
             if n < 10:
                 i, j = PAIRS[n]
-                loc[m, half] = lax.dot_general(x_ref[:, 256 * i:256 * i + 256], x_ref[:, 256 * j:256 * j + 256],
-                                               (((0,), (0,)), ((), ())), preferred_element_type=F32)
+                keep(m, half, lax.dot_general(x_ref[:, 256 * i:256 * i + 256], x_ref[:, 256 * j:256 * j + 256],
+                                              (((0,), (0,)), ((), ())), preferred_element_type=F32))
             elif n == 10:
                 me = ((at["y"] * 2 + core) * 4 + at["x"]) * 4 + at["z"]
-                where = lax.broadcasted_iota(jnp.int32, (32, 2048), 1)
-                hit = (where == prow_ref[...]) & (pdev_ref[...] == me)
-                picked = dot(hit.astype(F32).astype(BF16), x_ref[...], NN)
-                for part in range(4):
-                    loc[m, half, 32 * part:32 * part + 32, :] = picked[:, 256 * part:256 * part + 256]
-                loc[m, half, 128:256, :] = jnp.zeros((128, 256), F32)
+                pivot = lax.broadcasted_iota(jnp.int32, (32, 128), 0)
+                lane = lax.broadcasted_iota(jnp.int32, (32, 128), 1)
+                target = jnp.full((32, 128), -1, jnp.int32)
+                for i in range(32):
+                    target = jnp.where(pivot == i, jnp.where(pdev_ref[i] == me, prow_ref[i], -1), target)
+                hit = jnp.concatenate([(target == lane + 128 * i).astype(F32).astype(BF16) for i in range(16)], axis=1)
+                picked = dot(hit, x_ref[...], NN)
+                keep(m, half, jnp.concatenate([picked[:, 256 * part:256 * part + 256] for part in range(4)]
+                                              + [jnp.zeros((128, 256), F32)], axis=0))
             else:
-                loc[m, half] = jnp.zeros((256, 256), F32)
-        swaps[m] = go(remote(loc.at[m, other], r0.at[m], send0.at[m], recv0.at[m], "core", other))
-
-    def offsets(axis):
-        return [(d, lax.rem(at[axis] + d, 4)) for d in (1, 2, 3)]
-
-    down, up = {}, {}
-
-    def down1(c):
-        for m in (2 * c, 2 * c + 1):
-            swaps[m].wait_recv()
-            total = loc[m, core] + r0[m]
-            acc[c, 2 * (m % 2)] = total[:128]
-            acc[c, 2 * (m % 2) + 1] = total[128:]
-        axis = TURNS[c][0]
-        down[0, c] = [go(remote(acc.at[c, p], r1.at[c, d - 1], send_down.at[0, c, d - 1], recv_down.at[0, c, d - 1], axis, p))
-                      for d, p in offsets(axis)]
-
-    def down2(c):
-        for copy in down[0, c]:
+                keep(m, half, jnp.zeros((256, 256), F32))
+
+    swaps, down, across, back, up, over = {}, {}, {}, {}, {}, []
+
+    def swap(m):
+        swaps[m] = go(loc.at[m, other], r0.at[m], send0.at[m], recv0.at[m], {"core": other})
+
+    def down1(m):
+        swaps[m].wait_recv()
+        for i in range(2):
+            total = loc[m, core, i] + r0[m, i]
+            acc[m, 2 * i] = total[:128]
+            acc[m, 2 * i + 1] = total[128:]
+        axis = TURNS[m % 3][0]
+        down[m] = [go(acc.at[m, peer[axis]], r1.at[m, slot], send1.at[m, slot], recv1.at[m, slot], peer)
+                   for slot, peer in axis_peers(axis)]
+
+    def down2(m):
+        for copy in down[m]:
             copy.wait_recv()
-        total = (acc[c, at[TURNS[c][0]]] + r1[c, 0]) + (r1[c, 1] + r1[c, 2])
-        for i in range(4):
-            a1[c, i] = total[32 * i:32 * i + 32]
-        axis = TURNS[c][1]
-        down[1, c] = [go(remote(a1.at[c, p], r2.at[c, d - 1], send_down.at[1, c, d - 1], recv_down.at[1, c, d - 1], axis, p))
-                      for d, p in offsets(axis)]
-
-    def down3(c):
-        for copy in down[1, c]:
+        total = (acc[m, at[TURNS[m % 3][0]]] + r1[m, 0]) + (r1[m, 1] + r1[m, 2])
+        for i in range(16):
+            a1[m, i // 4, i % 4] = total[8 * i:8 * i + 8]
+        one, two = TURNS[m % 3][1:]
+        across[m] = [go(a1.at[m, peer[one], peer[two]], r2.at[m, slot], send2.at[m, slot], recv2.at[m, slot], peer)
+                     for slot, peer in plane_peers(m)]
+
+    def up2(m):
+        for copy in across[m]:
             copy.wait_recv()
-        total = (a1[c, at[TURNS[c][1]]] + r2[c, 0]) + (r2[c, 1] + r2[c, 2])
-        for i in range(4):
-            a2[c, i] = total[8 * i:8 * i + 8]
-        axis = TURNS[c][2]
-        down[2, c] = [go(remote(a2.at[c, p], r3.at[c, d - 1], send_down.at[2, c, d - 1], recv_down.at[2, c, d - 1], axis, p))
-                      for d, p in offsets(axis)]
-
-    def up3(c):
-        for copy in down[2, c]:
+        one, two, three = (at[name] for name in TURNS[m % 3])
+        terms = [a1[m, two, three]] + [r2[m, slot] for slot in range(15)]
+        while len(terms) > 1:
+            terms = [terms[i] + terms[i + 1] for i in range(0, len(terms), 2)]
+        out_ref[core, m, one, two, three] = terms[0]
+        mine = out_ref.at[core, m, one, two, three]
+        back[m] = [go(mine, mine, send3.at[m, slot], recv3.at[m, slot], peer) for slot, peer in plane_peers(m)]
+
+    def up1(m):
+        for copy in back[m]:
             copy.wait_recv()
-        one, two, three = (at[name] for name in TURNS[c])
-        out_ref[core, c, one, two, three] = (a2[c, three] + r3[c, 0]) + (r3[c, 1] + r3[c, 2])
-        mine = out_ref.at[core, c, one, two, three]
-        axis = TURNS[c][2]
-        up[2, c] = [go(remote(mine, mine, send_up.at[2, c, d - 1], recv_up.at[2, c, d - 1], axis, p)) for d, p in offsets(axis)]
-
-    def up2(c):
-        for copy in up[2, c]:
-            copy.wait_recv()
-        one, two, three = (at[name] for name in TURNS[c])
-        mine = out_ref.at[core, c, one, two]
-        axis = TURNS[c][1]
-        up[1, c] = [go(remote(mine, mine, send_up.at[1, c, d - 1], recv_up.at[1, c, d - 1], axis, p)) for d, p in offsets(axis)]
-
-    def up1(c):
-        for copy in up[1, c]:
-            copy.wait_recv()
-        one, two, three = (at[name] for name in TURNS[c])
-        mine = out_ref.at[core, c, one]
-        axis = TURNS[c][0]
-        up[0, c] = [go(remote(mine, mine, send_up.at[0, c, d - 1], recv_up.at[0, c, d - 1], axis, p)) for d, p in offsets(axis)]
-
-    def last(c):
-        for copy in up[0, c]:
-            copy.wait_recv()
-        mine = out_ref.at[core, c]
-        up[3, c] = go(remote(mine, mine, send4.at[c], recv4.at[c], "core", other))
-
-    pair(0)
-    pair(1)
-    pair(2)
+        axis = TURNS[m % 3][0]
+        mine = out_ref.at[core, m, at[axis]]
+        up[m] = [go(mine, mine, send4.at[m, slot], recv4.at[m, slot], peer) for slot, peer in axis_peers(axis)]
+        over.append(go(mine, mine, send5.at[m, 3], recv5.at[m, 3], {"core": other}))
+
+    def forward(m, slot):
+        up[m][slot].wait_recv()
+        piece = out_ref.at[core, m, lax.rem(at[TURNS[m % 3][0]] + 3 - slot, 4)]
+        over.append(go(piece, piece, send5.at[m, slot], recv5.at[m, slot], {"core": other}))
+
+    early, late = (0, 1, 2), (3, 4, 5)
+    for m in early:
+        for slab in slabs[2 * m:2 * m + 2]:
+            slab.wait()
+        pair(m)
+    pl.semaphore_wait(barrier, 37)
+    for m in early:
+        swap(m)
     pair(3)
-    down1(0)
+    swap(3)
+    for m in early:
+        down1(m)
     pair(4)
+    swap(4)
     pair(5)
-    down1(1)
-    down1(2)
-    for stage in (down2, down3, up3, up2, up1, last):
-        for c in range(3):
-            stage(c)
-    for c in range(3):
-        up[3, c].wait_recv()
+    swap(5)
+    for stage, units in ((down1, late), (down2, early), (down2, late), (up2, early), (up2, late), (up1, early), (up1, late)):
+        for m in units:
+            stage(m)
+    for units in (early, late):
+        for slot in (0, 2, 1):
+            for m in units:
+                forward(m, slot)
+    for copy in over:
+        copy.wait_recv()
     for copy in sent:
         copy.wait_send()
 
 
 def reduce_call(x, pdev, prow):
+    dma = pltpu.SemaphoreType.DMA
     return pl.pallas_call(
         reduce_kernel,
-        out_shape=jax.ShapeDtypeStruct((2, 3, 4, 4, 4, 8, 256), F32),
-        in_specs=[pl.BlockSpec(memory_space=pltpu.VMEM)] * 3,
+        out_shape=jax.ShapeDtypeStruct((2, 6, 4, 4, 4, 8, 128), F32),
+        in_specs=[pl.BlockSpec(memory_space=pltpu.HBM)] + [pl.BlockSpec(memory_space=pltpu.SMEM)] * 2,
         out_specs=pl.BlockSpec(memory_space=pltpu.VMEM),
         scratch_shapes=[
-            pltpu.VMEM((6, 2, 256, 256), F32), pltpu.VMEM((6, 256, 256), F32), pltpu.VMEM((3, 4, 128, 256), F32),
-            pltpu.VMEM((3, 3, 128, 256), F32), pltpu.VMEM((3, 4, 32, 256), F32),
-            pltpu.VMEM((3, 3, 32, 256), F32), pltpu.VMEM((3, 4, 8, 256), F32), pltpu.VMEM((3, 3, 8, 256), F32),
-            pltpu.SemaphoreType.DMA((6,)), pltpu.SemaphoreType.DMA((6,)),
-            pltpu.SemaphoreType.DMA((3, 3, 3)), pltpu.SemaphoreType.DMA((3, 3, 3)),
-            pltpu.SemaphoreType.DMA((3, 3, 3)), pltpu.SemaphoreType.DMA((3, 3, 3)),
-            pltpu.SemaphoreType.DMA((3,)), pltpu.SemaphoreType.DMA((3,)),
+            pltpu.VMEM((2048, 1024), BF16),
+            pltpu.VMEM((6, 2, 2, 256, 128), F32), pltpu.VMEM((6, 2, 256, 128), F32), pltpu.VMEM((6, 4, 128, 128), F32),
+            pltpu.VMEM((6, 3, 128, 128), F32), pltpu.VMEM((6, 4, 4, 8, 128), F32), pltpu.VMEM((6, 15, 8, 128), F32),
+            dma((4,)), dma((6,)), dma((6,)), dma((6, 3)), dma((6, 3)), dma((6, 15)), dma((6, 15)),
+            dma((6, 15)), dma((6, 15)), dma((6, 3)), dma((6, 3)), dma((6, 4)), dma((6, 4)),
         ],
-        compiler_params=pltpu.CompilerParams(vmem_limit_bytes=48 * 1024 * 1024, collective_id=0, has_side_effects=True),
+        compiler_params=pltpu.CompilerParams(vmem_limit_bytes=56 * 1024 * 1024, collective_id=0, has_side_effects=True),
         name="gram_sum",
     )(x, pdev, prow)
 
@@ -245,7 +256,7 @@
     load = pltpu.make_async_copy(x_hbm, x_ref, x_sem)
     load.start()
     for n, (i, j) in enumerate(PAIRS):
-        block = b_ref[n % 2, n // 2]
+        block = jnp.concatenate([b_ref[n % 2, n // 2, 0], b_ref[n % 2, n // 2, 1]], axis=1)
         hi, lo = split(block)
         gh[pl.ds(256 * i, 256), pl.ds(256 * j, 256)] = hi
         gl[pl.ds(256 * i, 256), pl.ds(256 * j, 256)] = lo
@@ -351,7 +362,8 @@
 
     coef = zf[...]
     for part in range(4):
-        xs = b_ref[0, 5, pl.ds(32 * part, 32), :].astype(BF16)
+        here = pl.ds(32 * part, 32)
+        xs = jnp.concatenate([b_ref[0, 5, 0, here, :], b_ref[0, 5, 1, here, :]], axis=1).astype(BF16)
         term = dot(xs, coef[:, 256 * part:256 * (part + 1)], NT)
         panel = term if part == 0 else panel + term
     ph = split(panel)
@@ -370,7 +382,7 @@
 
     inv = split(inverse_factors([small], 4, 32)[0][:, :32])
     pbt = dot3(inv, ph, NN)
-    pb_ref[...] = pbt.T
+    pb_ref[...] = pbt
     pb = split(pbt.T)
     proj = split(dot3(pb, pb, NT))
     ones = jnp.ones((8, 256), BF16)
@@ -380,7 +392,8 @@
         remaining = basis - dot3(split(basis), proj, NN)
         hi, lo = split(remaining * remaining)
         total = dot(ones, hi, NT) + dot(ones, lo, NT)
-        scores_ref[n:n + 1, :] = total[:1] * (1.0 / 256)
+        scores_ref[2 * n:2 * n + 1, :] = total[:1, :128] * (1.0 / 256)
+        scores_ref[2 * n + 1:2 * n + 2, :] = total[:1, 128:] * (1.0 / 256)
     for copy in stores:
         copy.wait()
 
@@ -391,8 +404,8 @@
     rows = x.shape[0]
     return pl.pallas_call(
         functools.partial(iterate_kernel, inv_rows),
-        out_shape=(jax.ShapeDtypeStruct((rows, 256), BF16), jax.ShapeDtypeStruct((8, 256), F32),
-                   jax.ShapeDtypeStruct((256, 32), F32)),
+        out_shape=(jax.ShapeDtypeStruct((rows, 256), BF16), jax.ShapeDtypeStruct((rows // 128, 128), F32),
+                   jax.ShapeDtypeStruct((32, 256), F32)),
         in_specs=[vmem(), vmem(), hbm()],
         out_specs=(hbm(), vmem(), vmem()),
         scratch_shapes=[
@@ -407,16 +420,16 @@
             pltpu.VMEM((rows, 1024), BF16), pltpu.VMEM((rows, 256), BF16), pltpu.VMEM((rows, 256), F32),
             pltpu.SemaphoreType.DMA, pltpu.SemaphoreType.DMA((8,)),
         ],
-        compiler_params=pltpu.CompilerParams(vmem_limit_bytes=56 * 1024 * 1024),
+        compiler_params=pltpu.CompilerParams(vmem_limit_bytes=50 * 1024 * 1024),
         name="iterate",
     )(packed, start, x)
 
 
 def local(snapshots, start, pivot_dev, pivot_row):
     rows_total = snapshots.shape[0] * lax.axis_size(AXES)
-    packed = reduce_call(snapshots, pivot_dev[:, None], pivot_row[:, None])
-    modes, scores, panel_basis = iterate_call(packed.reshape(2, 6, 256, 256), start, snapshots, 1.0 / rows_total)
-    return (modes, scores.reshape(-1), panel_basis)
+    packed = reduce_call(snapshots, pivot_dev, pivot_row)
+    modes, scores, panel_basis = iterate_call(packed.reshape(2, 6, 2, 256, 128), start, snapshots, 1.0 / rows_total)
+    return (modes, scores.reshape(-1), panel_basis.T)
 
 
 def solution(mesh):

time: 99.8 us -> 88.3 us (0.88)
  local copies, waits for them, and re-layouts: 6.02 us -> 0.01 us
  Pallas kernels: 92.9 us -> 87.2 us
    pallas_call x1, Pallas kernels: 48.9 us -> 43.6 us  [reduce_call(): pl.pallas_call(reduce_kernel, out_shape=jax.ShapeDtypeStruct((2, 6, 4, 4,...]
    unnamed x4 -> x2, local copies, waits for them, and re-layouts: 4.54 us -> 0.01 us
    broadcast_in_dim x2 -> x0, local copies, waits for them, and re-layouts: 1.47 us -> none  [local(): packed = reduce_call(snapshots, pivot_dev[:, None], pivot_row[:, None])]
where the time goes in v3:
time: 88.3 us; the launch traced here: 88.1 us
  Pallas kernels  87.2 us (99%)
    pallas_call x1, Pallas kernels, reduce_call(): pl.pallas_call(reduce_kernel, out_shape=jax.ShapeDtypeStruct((2, 6, 4, 4,...  43.6 us
    pallas_call x1, Pallas kernels, iterate_call(): pl.pallas_call(functools.partial(iterate_kernel, inv_rows), out_shape=(ja...  43.6 us

profile of v3, /device:TPU:1, one launch (start us, length us, event | category | flops | bytes accessed | tf_op | source)
XLA Modules:
  0.0 88.1 jit_solution(6031675684897504468)
XLA Ops:
  0.6 0.0 copy-start
  0.6 43.6 %gram_sum.1 = f32[2,6,4,4,4,8,128]{6,5,4,3,2,1,0:T(8,128)} custom-call(bf16[2048,1024]{1,0:T(8,128)(2,1)} %x_hbm.3, s32[32]{0:T(128)} %pdev_ref.1, s32[32]{0:T(128)} %prow_ref.1), custom_call_target="tpu_custom_call" | custom-call | tf_op jit(solution)/shard_map/gram_sum/pallas_call | solution.py:179
  44.3 0.0 copy-done
  44.3 43.6 %iterate.1 = (bf16[2048,256]{1,0:T(8,128)(2,1)}, f32[16,128]{1,0:T(8,128)}, f32[32,256]{1,0:T(8,128)}) custom-call(f32[2,6,2,256,128]{4,3,2,1,0:T(8,128)} %bitcast.3, f32[1024,256]{1,0:T(8,128)S(1)} %copy-done, bf16[2048,1024]{1,0:T(8,128)(2,1)} %x_hbm.3), custom_call_target="tpu_custom_call" | custom-call | tf_op jit(solution)/shard_map/iterate/pallas_call | solution.py:405
Async XLA Ops:
  0.6 43.7 %copy-start = (f32[1024,256]{1,0:T(8,128)S(1)}, f32[1024,256]{1,0:T(8,128)}, u32[]{:S(2)}) copy-start(f32[1024,256]{1,0:T(8,128)} %start_ref.1) | copy-start | bytes 3145732

commit v4 on v3

--- a/solution.py
+++ b/solution.py
@@ -297,10 +297,11 @@
         for k, j in tasks:
             scale = inv_rows if k == 4 else 1.0
             a = left(k, block(j))
-            ds[k] = stacked3(a, (yh[k, block(j), :], yl[k, block(j), :]), NT) * scale
+            upto = pl.ds(0, NB * (j + 1))
+            both = stacked3(a, (yh[k, upto, :], yl[k, upto, :]), NT) * scale
+            ds[k] = both[:, NB * j:]
             if j > 0:
-                before = pl.ds(0, NB * j)
-                ms[k] = split(stacked3(a, (yh[k, before, :], yl[k, before, :]), NT) * scale)
+                ms[k] = split(both[:, :NB * j])
         for k, j in tasks:
             if j > 0:
                 before = pl.ds(0, NB * j)

time: 88.3 us -> 87.5 us (level)
  no operation moved by 1% of the time
where the time goes in v4:
time: 87.5 us; the launch traced here: 87.3 us
  Pallas kernels  86.4 us (99%)
    pallas_call x1, Pallas kernels, reduce_call(): pl.pallas_call(reduce_kernel, out_shape=jax.ShapeDtypeStruct((2, 6, 4, 4,...  43.6 us
    pallas_call x1, Pallas kernels, iterate_call(): pl.pallas_call(functools.partial(iterate_kernel, inv_rows), out_shape=(ja...  42.8 us

profile of v4, /device:TPU:1, one launch (start us, length us, event | category | flops | bytes accessed | tf_op | source)
XLA Modules:
  0.0 87.3 jit_solution(12604084671032647151)
XLA Ops:
  0.6 0.0 copy-start
  0.6 43.6 %gram_sum.1 = f32[2,6,4,4,4,8,128]{6,5,4,3,2,1,0:T(8,128)} custom-call(bf16[2048,1024]{1,0:T(8,128)(2,1)} %x_hbm.3, s32[32]{0:T(128)} %pdev_ref.1, s32[32]{0:T(128)} %prow_ref.1), custom_call_target="tpu_custom_call" | custom-call | tf_op jit(solution)/shard_map/gram_sum/pallas_call | solution.py:179
  44.3 0.0 copy-done
  44.3 42.8 %iterate.1 = (bf16[2048,256]{1,0:T(8,128)(2,1)}, f32[16,128]{1,0:T(8,128)}, f32[32,256]{1,0:T(8,128)}) custom-call(f32[2,6,2,256,128]{4,3,2,1,0:T(8,128)} %bitcast.3, f32[1024,256]{1,0:T(8,128)S(1)} %copy-done, bf16[2048,1024]{1,0:T(8,128)(2,1)} %x_hbm.3), custom_call_target="tpu_custom_call" | custom-call | tf_op jit(solution)/shard_map/iterate/pallas_call | solution.py:406
Async XLA Ops:
  0.6 43.7 %copy-start = (f32[1024,256]{1,0:T(8,128)S(1)}, f32[1024,256]{1,0:T(8,128)}, u32[]{:S(2)}) copy-start(f32[1024,256]{1,0:T(8,128)} %start_ref.1) | copy-start | bytes 3145732
